TPU v7x, 512 devices: a whole 4x4x16 slice. The times are simulated.
512 devices in a mesh: img: 8 (over y, x_lo), gz: 32 (over x_hi, z), gy: 2 (over core).
Axes of the slice: x: 4 (x_hi: 2, x_lo: 2; x = x_hi * 2 + x_lo), y: 4, z: 16, core: 2. Of those that a mesh axis runs over, the one named last changes fastest.
Arguments:
- pixels: bfloat16 [2, 48, 393216], P(None, None, ('img', 'gz', 'gy')), may hold values from -6 to 6
- taps: bfloat16 [9, 393216], P(None, ('img', 'gz', 'gy')), may hold values from 0.099609375 to 1
- plane_offset: int32 [393216], P(('img', 'gz', 'gy')), may hold values from 0 to 15
- grid_row: int32 [393216], P(('img', 'gz', 'gy')), may hold values from 0 to 511
- slab_of_block: int32 [24576, 1], P(('img', 'gz', 'gy')), may hold values from 0 to 31; in each aligned block of 48 rows (0 to 47, 48 to 95, ...) at most 3 rows name the same one
Outputs:
- volume: float32 [2, 48, 512, 512], P(None, ('img', 'gy'), 'gz')
Inputs may be any that keep to these rules, and one draw needn't show every extreme that they name: `slab_of_block`: within the 48 blocks of one device no slab is named by more than 3 blocks, and on some devices one slab is named by exactly 3 blocks.
All inputs are finite; a program needn't handle non-finite values.
Results may differ from a plain program's by a relative error of at most 0.004.
Values may be sent and summed in bfloat16 or wider, within the bound.
A program may use at most 64 MiB of HBM per device.

v0:
```python
import functools
import math

import jax
import jax.numpy as jnp
import numpy as np
from jax import lax
from jax.experimental import pallas as pl
from jax.experimental.pallas import tpu as pltpu
from jax.sharding import PartitionSpec as P

MESH = pl.DeviceIdType.MESH
F32 = jnp.float32
BF16 = jnp.bfloat16
TILE = 16
CAPACITY = 3
META = 8
LANES = 128
NT = (((1,), (1,)), ((), ()))


def transform_table(length):
    steps = np.arange(length)
    phase = (steps[:, None] * steps[None, :] % length) * (2.0 * math.pi / length)
    table = np.concatenate([np.cos(phase), np.sin(phase)], axis=1) / math.sqrt(length)
    table = table.astype(np.float32)
    high = table.astype(jnp.bfloat16)
    low = (table - high.astype(np.float32)).astype(jnp.bfloat16)
    return np.stack([high, low])


def pick_table(width, groups):
    columns = width // groups
    pick = np.zeros((groups, TILE, LANES), np.float32)
    for group in range(groups):
        for s in range(2 * columns):
            pick[group, s, (s % 2) * width + group * columns + s // 2] = 1.0
        for s in range(META):
            pick[group, 2 * columns + s, 2 * width + s] = 1.0
    return pick.reshape(groups * TILE, LANES).astype(jnp.bfloat16)


def rim_table(columns):
    place = np.zeros((LANES, LANES), np.float32)
    for x in range(columns):
        for c in range(2):
            for z in range(2):
                place[2 * columns * TILE + TILE * c + 2 * x + z, (2 * x + c) * TILE + z] = 1.0
    return place.astype(jnp.bfloat16)


def kernel(
    sizes, pix_ref, taps_ref, plane_ref, row_ref, slab_ref, pick_ref, rim_ref, table_hbm, out_ref,
    x_buf, send1, recv1, send2, recv2, acc, table, send3, recv3,
    s1_sem, r1_sem, s2_sem, r2_sem, s3_sem, r3_sem, table_sem,
):
    n_img, n_gz, n_gy, width, ny, parts, step = sizes
    nx_hi = 2
    nz = n_gz // nx_hi
    groups = n_img * n_gy
    columns = width // groups
    rows = pix_ref.shape[2]
    blocks = rows // TILE
    slot_rows = CAPACITY * TILE
    part_slots = n_gz // parts
    part_rows = part_slots * slot_rows
    half = ny // 2

    img, gz, gy = lax.axis_index("img"), lax.axis_index("gz"), lax.axis_index("gy")
    my_group = img * n_gy + gy

    def slab_peer(k):
        turn, m = k % nx_hi, k // nx_hi
        along = ((m + 1) // 2) * (2 * (m % 2) - 1)
        z = (gz % nz + along + nz) % nz
        x = (gz // nz + turn) % nx_hi
        return x * nz + z

    def group_peer(e):
        core, rest = e % n_gy, e // n_gy
        side, along = rest % 2, rest // 2
        y = (img // 2 + along) % (n_img // 2)
        x = (img % 2 + side) % 2
        return y * 2 + x, (gy + core) % n_gy

    def copy1(k):
        peer = slab_peer(k)
        return pltpu.make_async_remote_copy(
            src_ref=send1.at[pl.ds(pl.multiple_of(peer * slot_rows, TILE), slot_rows)],
            dst_ref=recv1.at[pl.ds(pl.multiple_of(k * slot_rows, TILE), slot_rows)],
            send_sem=s1_sem.at[k], recv_sem=r1_sem.at[k],
            device_id=(img, peer, gy), device_id_type=MESH,
        )

    def copy2(part, e):
        to_img, to_gy = group_peer(e)
        peer = to_img * n_gy + to_gy
        return pltpu.make_async_remote_copy(
            src_ref=send2.at[part, pl.ds(pl.multiple_of(peer * TILE, TILE), TILE)],
            dst_ref=recv2.at[part, e],
            send_sem=s2_sem.at[part, e], recv_sem=r2_sem.at[part, e],
            device_id=(to_img, gz, to_gy), device_id_type=MESH,
        )

    def copy3(k):
        peer = slab_peer(k)
        return pltpu.make_async_remote_copy(
            src_ref=send3.at[pl.ds(pl.multiple_of(peer * TILE, TILE), TILE)],
            dst_ref=recv3.at[pl.ds(pl.multiple_of(gz * TILE, TILE), TILE)],
            send_sem=s3_sem.at[k], recv_sem=r3_sem.at[k],
            device_id=(img, peer, gy), device_id_type=MESH,
        )

    def loop(first, last, do):
        def body(index, carry):
            do(index)
            return carry
        lax.fori_loop(first, last, body, 0)

    barrier = pltpu.get_barrier_semaphore()

    def greet_slab(k):
        pl.semaphore_signal(barrier, inc=1, device_id=(img, slab_peer(k), gy), device_id_type=MESH)

    def greet_group(e):
        to_img, to_gy = group_peer(e)
        pl.semaphore_signal(barrier, inc=1, device_id=(to_img, gz, to_gy), device_id_type=MESH)

    loop(1, n_gz, greet_slab)
    loop(1, groups, greet_group)

    table_copy = pltpu.make_async_copy(table_hbm, table, table_sem)
    table_copy.start()

    taps = taps_ref[...].astype(F32)
    x_iota = lax.broadcasted_iota(jnp.int32, (width, rows), 0)
    for c in range(2):
        p = pix_ref[c].astype(F32)
        before = jnp.where(x_iota == 0, 0.0, pltpu.roll(p, 1, 0))
        after = jnp.where(x_iota == width - 1, 0.0, pltpu.roll(p, width - 1, 0))
        spread = taps[6:7] * before + taps[7:8] * p + taps[8:9] * after
        x_buf[c * width : (c + 1) * width] = spread.astype(BF16)
    data = jnp.concatenate(
        [
            taps[0:6], plane_ref[...].astype(F32), (row_ref[...] - half).astype(F32),
            jnp.zeros((LANES - 2 * width - META, rows), F32),
        ],
        axis=0,
    )
    x_buf[2 * width :] = data.astype(BF16)

    block_iota = lax.broadcasted_iota(jnp.int32, (blocks, rows), 0)
    row_iota = lax.broadcasted_iota(jnp.int32, (blocks, rows), 1)
    row_block = row_iota // TILE
    target = jnp.broadcast_to(slab_ref[...], (blocks, rows))
    own = jnp.sum(jnp.where(block_iota == row_block, target, 0), axis=0, keepdims=True)
    earlier = jnp.where((target == own) & (block_iota < row_block), 1, 0)
    rank = jnp.sum(earlier, axis=0, keepdims=True)
    place = (own * CAPACITY + rank) * TILE + row_iota[0:1] % TILE

    slot_iota = lax.broadcasted_iota(jnp.int32, (LANES, rows), 0)

    def permute(index):
        first = pl.multiple_of(index * LANES, LANES)
        chosen = jnp.where(slot_iota == place - first, 1.0, 0.0).astype(BF16)
        moved = lax.dot_general(chosen, x_buf[...], NT, preferred_element_type=F32)
        send1[pl.ds(first, LANES)] = moved.astype(BF16)

    loop(0, n_gz * slot_rows // LANES, permute)

    pl.semaphore_wait(barrier, n_gz + groups - 2)
    loop(1, n_gz, lambda k: copy1(k).start())
    recv1[0:slot_rows] = send1[pl.ds(pl.multiple_of(gz * slot_rows, TILE), slot_rows)]

    acc[...] = jnp.zeros_like(acc)
    y_iota = lax.broadcasted_iota(jnp.int32, (half + TILE, step), 0).astype(F32)
    z_iota = lax.broadcasted_iota(jnp.int32, (TILE, step), 0)
    rim_x = z_iota // 2
    rim_z = (z_iota % 2 + TILE).astype(F32)
    z_iota = z_iota.astype(F32)

    def spread_part(part, index):
        e, first = index // (part_rows // step), index % (part_rows // step)
        got = recv2[part, e, :, pl.ds(pl.multiple_of(first * step, step), step)].astype(F32)
        plane = got[12:13]
        y = got[13:14] + (half - 1.0)
        y = jnp.where(y < 0.0, y + ny, y)
        upper = y >= half
        y = jnp.where(upper, y - half, y)
        along_y = jnp.where(
            y_iota == y, got[9:10],
            jnp.where(y_iota == y + 1.0, got[10:11], jnp.where(y_iota == y + 2.0, got[11:12], 0.0)),
        ).astype(BF16)
        along_z = jnp.where(
            z_iota == plane, got[6:7],
            jnp.where(
                z_iota == plane + 1.0, got[7:8], jnp.where(z_iota == plane + 2.0, got[8:9], 0.0)
            ),
        )
        rim = jnp.where(
            rim_z == plane + 1.0, got[7:8], jnp.where(rim_z == plane + 2.0, got[8:9], 0.0)
        )
        pieces = [along_z * got[s : s + 1] for s in range(2 * columns)]
        for c in range(2):
            value = jnp.zeros((TILE, step), F32)
            for x in range(columns):
                value = jnp.where(rim_x == x, got[2 * x + c : 2 * x + c + 1], value)
            pieces.append(rim * value)
        pieces = [jnp.where(upper, 0.0, piece) for piece in pieces] + [
            jnp.where(upper, piece, 0.0) for piece in pieces
        ]
        along_zx = jnp.concatenate([piece.astype(BF16) for piece in pieces], axis=0)
        acc[...] += lax.dot_general(along_y, along_zx, NT, preferred_element_type=F32)

    def take_part(part):
        def arrived(k):
            copy1(k).wait_recv()
        loop(jnp.maximum(part * part_slots, 1), (part + 1) * part_slots, arrived)
        first = pl.multiple_of(part * part_rows, TILE)
        turned = lax.dot_general(
            pick_ref[...], recv1[pl.ds(first, part_rows)], NT, preferred_element_type=F32
        )
        send2[part] = turned.astype(BF16)
        loop(1, groups, lambda e: copy2(part, e).start())
        recv2[part, 0] = send2[part, pl.ds(pl.multiple_of(my_group * TILE, TILE), TILE)]

    def grid_part(part):
        loop(1, groups, lambda e: copy2(part, e).wait_recv())
        loop(0, groups * part_rows // step, functools.partial(spread_part, part))

    def pipeline(part):
        take_part(part)
        grid_part(part - 1)

    take_part(0)
    loop(1, parts, pipeline)
    grid_part(parts - 1)

    table_copy.wait()
    lane = lax.broadcasted_iota(jnp.int32, (ny, LANES), 1)
    low, high = acc[:half, :LANES], acc[:half, LANES:]
    low_rim, high_rim = acc[half:, :LANES], acc[half:, LANES:]
    grid = jnp.concatenate(
        [low[:TILE] + high_rim, low[TILE:], high[:TILE] + low_rim, high[TILE:]], axis=0
    )
    other = jnp.where(
        (lane // TILE) % 2 == 0, -pltpu.roll(grid, LANES - TILE, 1), pltpu.roll(grid, TILE, 1)
    )
    both = jnp.concatenate([grid, other], axis=0)
    both_high = both.astype(BF16)
    both_low = (both - both_high.astype(F32)).astype(BF16)
    both_bits = jnp.concatenate([both_high, both_low], axis=1)
    wide = jnp.dot(table[0], both_bits, preferred_element_type=F32)
    turned = wide[:, :LANES] + wide[:, LANES:]
    turned = turned + jnp.dot(table[1], both_high, preferred_element_type=F32)
    send3[...] = turned.astype(BF16)

    loop(1, n_gz, lambda k: copy3(k).start())
    here = pl.ds(pl.multiple_of(gz * TILE, TILE), TILE)
    recv3[here] = send3[here]
    loop(1, n_gz, lambda k: copy3(k).wait_recv())

    got = recv3[...]
    past = jnp.dot(got, rim_ref[...], preferred_element_type=F32)
    planes = got.astype(F32) + jnp.concatenate([past[-TILE:], past[:-TILE]], axis=0)
    per = LANES // TILE
    spot = lax.broadcasted_iota(jnp.int32, (TILE, LANES), 1) // TILE
    ordered = []
    for s in range(2 * columns):
        across = []
        for t in range(n_gz // per):
            value = jnp.zeros((TILE, LANES), F32)
            for j in range(per):
                first = (t * per + j) * TILE
                tile = planes[first : first + TILE]
                turn = (j - s) * TILE % LANES
                tile = pltpu.roll(tile, turn, 1) if turn else tile
                value = jnp.where(spot == j, tile, value)
            across.append(value.astype(BF16))
        ordered.append(jnp.concatenate(across, axis=1))
    ordered = jnp.concatenate(ordered, axis=0)
    volume = jnp.dot(ordered, table[0], preferred_element_type=F32)
    volume = volume + jnp.dot(ordered, table[1], preferred_element_type=F32)
    for x in range(columns):
        real = volume[2 * x * TILE : (2 * x + 1) * TILE]
        imag = volume[(2 * x + 1) * TILE : (2 * x + 2) * TILE]
        out_ref[0, x] = real[:, :ny] - imag[:, ny:]
        out_ref[1, x] = real[:, ny:] + imag[:, :ny]

    loop(1, n_gz, lambda k: copy1(k).wait_send())
    loop(0, parts, lambda part: loop(1, groups, lambda e: copy2(part, e).wait_send()))
    loop(1, n_gz, lambda k: copy3(k).wait_send())


def local(sizes, pixels, taps, plane_offset, grid_row, slab_of_block):
    n_img, n_gz, n_gy, width, ny, parts, step = sizes
    groups = n_img * n_gy
    columns = width // groups
    rows = pixels.shape[2]
    slots = n_gz * CAPACITY * TILE
    vmem = pl.BlockSpec(memory_space=pltpu.VMEM)
    return pl.pallas_call(
        functools.partial(kernel, sizes),
        out_shape=jax.ShapeDtypeStruct((2, columns, ny // n_gz, ny), F32),
        in_specs=[vmem] * 7 + [pl.BlockSpec(memory_space=pl.ANY)],
        out_specs=vmem,
        scratch_shapes=[
            pltpu.VMEM((LANES, rows), BF16),
            pltpu.VMEM((slots, LANES), BF16),
            pltpu.VMEM((slots, LANES), BF16),
            pltpu.VMEM((parts, groups * TILE, slots // parts), BF16),
            pltpu.VMEM((parts, groups, TILE, slots // parts), BF16),
            pltpu.VMEM((ny // 2 + TILE, 2 * LANES), F32),
            pltpu.VMEM((2, ny, 2 * ny), BF16),
            pltpu.VMEM((ny, LANES), BF16),
            pltpu.VMEM((ny, LANES), BF16),
            pltpu.SemaphoreType.DMA((n_gz,)),
            pltpu.SemaphoreType.DMA((n_gz,)),
            pltpu.SemaphoreType.DMA((parts, groups)),
            pltpu.SemaphoreType.DMA((parts, groups)),
            pltpu.SemaphoreType.DMA((n_gz,)),
            pltpu.SemaphoreType.DMA((n_gz,)),
            pltpu.SemaphoreType.DMA,
        ],
        compiler_params=pltpu.CompilerParams(
            collective_id=0, has_side_effects=True, vmem_limit_bytes=48 * 1024 * 1024
        ),
    )(
        pixels, taps, plane_offset.reshape(1, rows), grid_row.reshape(1, rows), slab_of_block,
        jnp.asarray(pick_table(width, groups)), jnp.asarray(rim_table(columns)),
        jnp.asarray(transform_table(ny)),
    )


def solution(mesh, width=48, ny=512, parts=4, step=384):
    sizes = (mesh.shape["img"], mesh.shape["gz"], mesh.shape["gy"], width, ny, parts, step)
    return jax.shard_map(
        functools.partial(local, sizes),
        mesh=mesh,
        in_specs=(
            P(None, None, ("img", "gz", "gy")),
            P(None, ("img", "gz", "gy")),
            P(("img", "gz", "gy")),
            P(("img", "gz", "gy")),
            P(("img", "gz", "gy"), None),
        ),
        out_specs=P(None, ("img", "gy"), "gz", None),
        check_vma=False,
    )
```

profile of v0, /device:TPU:1, one launch (start us, length us, event | category | flops | bytes accessed | tf_op | source)
XLA Modules:
  0.0 78.7 jit_solution(2000451985123951457)
XLA Ops:
  0.0 0.7 reshape.6.plane_ref
  0.7 0.7 reshape.7.row_ref
  1.4 0.7 copy.9.slab_ref
  2.1 0.0 copy-start
  2.1 1.6 %copy-done = bf16[2,512,1024]{2,1,0:T(8,128)(2,1)S(1)} copy-done((bf16[2,512,1024]{2,1,0:T(8,128)(2,1)S(1)}, bf16[2,512,1024]{2,1,0:T(8,128)(2,1)}, u32[]{:S(2)}) %copy-start) | copy-done | bytes 2097176
  3.7 0.0 copy-start.1
  3.7 0.9 %copy-done.1 = bf16[2,48,768]{2,1,0:T(8,128)(2,1)S(1)} copy-done((bf16[2,48,768]{2,1,0:T(8,128)(2,1)S(1)}, bf16[2,48,768]{2,1,0:T(8,128)(2,1)}, u32[]{:S(2)}) %copy-start.1) | copy-done | bytes 147480
  4.6 0.0 copy-start.2
  4.6 0.8 %copy-done.2 = bf16[256,128]{1,0:T(8,128)(2,1)S(1)} copy-done((bf16[256,128]{1,0:T(8,128)(2,1)S(1)}, bf16[256,128]{1,0:T(8,128)(2,1)}, u32[]{:S(2)}) %copy-start.2) | copy-done | bytes 65560
  5.5 0.0 copy-start.3
  5.5 0.8 copy-done.3
  6.2 0.0 copy-start.4
  6.2 0.7 copy-done.4
  7.0 71.1 %shard_map.82 = f32[2,3,16,512]{3,2,1,0:T(8,128)S(1)} custom-call(bf16[2,48,768]{2,1,0:T(8,128)(2,1)S(1)} %copy-done.1, bf16[9,768]{1,0:T(8,128)(2,1)S(1)} %copy-done.4, s32[1,768]{1,0:T(1,128)S(1)} %reshape.6.plane_ref, s32[1,768]{1,0:T(1,128)S(1)} %reshape.7.row_ref, s32[48,1]{1,0:T(8,128)S(1)} %copy.9.slab_ref, bf16[256,128]{1,0:T(8,128)(2,1)S(1)} %copy-done.2, ...), custom_call_target="tpu_custom_call" | custom-call | tf_op jit(solution)/shard_map/pallas_call | solution.py:302
  78.1 0.7 copy.11
Async XLA Ops:
  2.1 1.6 %copy-start = (bf16[2,512,1024]{2,1,0:T(8,128)(2,1)S(1)}, bf16[2,512,1024]{2,1,0:T(8,128)(2,1)}, u32[]{:S(2)}) copy-start(bf16[2,512,1024]{2,1,0:T(8,128)(2,1)} %constant.8.clone.table_hbm) | copy-start | bytes 6291460
  3.7 0.9 %copy-start.1 = (bf16[2,48,768]{2,1,0:T(8,128)(2,1)S(1)}, bf16[2,48,768]{2,1,0:T(8,128)(2,1)}, u32[]{:S(2)}) copy-start(bf16[2,48,768]{2,1,0:T(8,128)(2,1)} %pix_ref.1) | copy-start | bytes 442372
  4.6 0.8 %copy-start.2 = (bf16[256,128]{1,0:T(8,128)(2,1)S(1)}, bf16[256,128]{1,0:T(8,128)(2,1)}, u32[]{:S(2)}) copy-start(bf16[256,128]{1,0:T(8,128)(2,1)} %constant.6.clone.pick_ref) | copy-start | bytes 196612
  5.5 0.8 copy-start.3
  6.2 0.7 copy-start.4
where the time goes:
time: 79.1 us; the launch traced here: 78.7 us
  Pallas kernels  71.1 us (90%)
  local copies, waits for them, and re-layouts  7.63 us (10%)
    pallas_call x1, Pallas kernels, local(): pl.pallas_call(functools.partial(kernel, sizes), out_shape=jax.ShapeDtype...  71.1 us
    unnamed x12, local copies, waits for them, and re-layouts  6.25 us

commit v1 on v0

--- a/solution.py
+++ b/solution.py
@@ -50,26 +50,28 @@
 
 
 def kernel(
-    sizes, pix_ref, taps_ref, plane_ref, row_ref, slab_ref, pick_ref, rim_ref, table_hbm, out_ref,
-    x_buf, send1, recv1, send2, recv2, acc, table, send3, recv3,
-    s1_sem, r1_sem, s2_sem, r2_sem, s3_sem, r3_sem, table_sem,
+    sizes, pix_hbm, taps_hbm, plane_hbm, row_hbm, slab_hbm, small_hbm, table_hbm, out_ref,
+    pix_ref, taps_ref, plane_ref, row_ref, slab_ref, small, x_buf, send1, recv1, send2, recv2, acc, table, send3, recv3,
+    s1_sem, r1_sem, s2_sem, r2_sem, s3_sem, r3_sem, in_sem,
 ):
     n_img, n_gz, n_gy, width, ny, parts, step = sizes
     nx_hi = 2
     nz = n_gz // nx_hi
     groups = n_img * n_gy
     columns = width // groups
-    rows = pix_ref.shape[2]
+    rows = pix_hbm.shape[2]
     blocks = rows // TILE
     slot_rows = CAPACITY * TILE
     part_slots = n_gz // parts
     part_rows = part_slots * slot_rows
     half = ny // 2
+    FAR, FIRST, LAST, OWN = True, 0, n_gz - 1, n_gz - 1
 
     img, gz, gy = lax.axis_index("img"), lax.axis_index("gz"), lax.axis_index("gy")
     my_group = img * n_gy + gy
 
     def slab_peer(k):
+        k = n_gz - 1 - k if FAR else k
         turn, m = k % nx_hi, k // nx_hi
         along = ((m + 1) // 2) * (2 * (m % 2) - 1)
         z = (gz % nz + along + nz) % nz
@@ -86,7 +88,7 @@
     def copy1(k):
         peer = slab_peer(k)
         return pltpu.make_async_remote_copy(
-            src_ref=send1.at[pl.ds(pl.multiple_of(peer * slot_rows, TILE), slot_rows)],
+            src_ref=send1.at[pl.ds(pl.multiple_of(k * slot_rows, TILE), slot_rows)],
             dst_ref=recv1.at[pl.ds(pl.multiple_of(k * slot_rows, TILE), slot_rows)],
             send_sem=s1_sem.at[k], recv_sem=r1_sem.at[k],
             device_id=(img, peer, gy), device_id_type=MESH,
@@ -97,17 +99,17 @@
         peer = to_img * n_gy + to_gy
         return pltpu.make_async_remote_copy(
             src_ref=send2.at[part, pl.ds(pl.multiple_of(peer * TILE, TILE), TILE)],
-            dst_ref=recv2.at[part, e],
+            dst_ref=recv2.at[part, :, pl.ds(pl.multiple_of(e * part_rows, LANES), part_rows)],
             send_sem=s2_sem.at[part, e], recv_sem=r2_sem.at[part, e],
             device_id=(to_img, gz, to_gy), device_id_type=MESH,
         )
 
-    def copy3(k):
-        peer = slab_peer(k)
+    def copy3(index):
+        peer = index % nx_hi * nz + index // nx_hi
         return pltpu.make_async_remote_copy(
             src_ref=send3.at[pl.ds(pl.multiple_of(peer * TILE, TILE), TILE)],
             dst_ref=recv3.at[pl.ds(pl.multiple_of(gz * TILE, TILE), TILE)],
-            send_sem=s3_sem.at[k], recv_sem=r3_sem.at[k],
+            send_sem=s3_sem.at[peer], recv_sem=r3_sem.at[gz],
             device_id=(img, peer, gy), device_id_type=MESH,
         )
 
@@ -117,6 +119,28 @@
             return carry
         lax.fori_loop(first, last, body, 0)
 
+    pairs = [
+        (slab_hbm, slab_ref), (taps_hbm, taps_ref), (plane_hbm, plane_ref), (row_hbm, row_ref),
+        (pix_hbm, pix_ref), (small_hbm, small), (table_hbm, table),
+    ]
+    fetches = [pltpu.make_async_copy(*pair, in_sem.at[i]) for i, pair in enumerate(pairs)]
+    for fetch in fetches:
+        fetch.start()
+
+    def arrival3(peer):
+        here = recv3.at[pl.ds(pl.multiple_of(peer * TILE, TILE), TILE)]
+        return pltpu.make_async_remote_copy(
+            src_ref=here, dst_ref=here, send_sem=s3_sem.at[0], recv_sem=r3_sem.at[peer],
+            device_id=(img, peer, gy), device_id_type=MESH,
+        )
+
+    def others(first, last, mine, do):
+        def step_of(index):
+            @pl.when(index != mine)
+            def _():
+                do(index)
+        loop(first, last, step_of)
+
     barrier = pltpu.get_barrier_semaphore()
 
     def greet_slab(k):
@@ -126,12 +150,12 @@
         to_img, to_gy = group_peer(e)
         pl.semaphore_signal(barrier, inc=1, device_id=(to_img, gz, to_gy), device_id_type=MESH)
 
-    loop(1, n_gz, greet_slab)
+    loop(FIRST, LAST, greet_slab)
     loop(1, groups, greet_group)
 
-    table_copy = pltpu.make_async_copy(table_hbm, table, table_sem)
-    table_copy.start()
-
+
+    for fetch in fetches[:5]:
+        fetch.wait()
     taps = taps_ref[...].astype(F32)
     x_iota = lax.broadcasted_iota(jnp.int32, (width, rows), 0)
     for c in range(2):
@@ -142,7 +166,8 @@
         x_buf[c * width : (c + 1) * width] = spread.astype(BF16)
     data = jnp.concatenate(
         [
-            taps[0:6], plane_ref[...].astype(F32), (row_ref[...] - half).astype(F32),
+            taps[0:6], plane_ref[...].reshape(1, rows).astype(F32),
+            (row_ref[...].reshape(1, rows) - half).astype(F32),
             jnp.zeros((LANES - 2 * width - META, rows), F32),
         ],
         axis=0,
@@ -152,77 +177,92 @@
     block_iota = lax.broadcasted_iota(jnp.int32, (blocks, rows), 0)
     row_iota = lax.broadcasted_iota(jnp.int32, (blocks, rows), 1)
     row_block = row_iota // TILE
-    target = jnp.broadcast_to(slab_ref[...], (blocks, rows))
+    square = (blocks, blocks)
+    diagonal = lax.broadcasted_iota(jnp.int32, square, 0) == lax.broadcasted_iota(jnp.int32, square, 1)
+    target = jnp.sum(jnp.where(diagonal, slab_ref[...], 0), axis=1, keepdims=True)
+    target = jnp.broadcast_to(target, (blocks, rows))
     own = jnp.sum(jnp.where(block_iota == row_block, target, 0), axis=0, keepdims=True)
     earlier = jnp.where((target == own) & (block_iota < row_block), 1, 0)
     rank = jnp.sum(earlier, axis=0, keepdims=True)
-    place = (own * CAPACITY + rank) * TILE + row_iota[0:1] % TILE
-
-    slot_iota = lax.broadcasted_iota(jnp.int32, (LANES, rows), 0)
+    turn = (own // nz - gz // nz + nx_hi) % nx_hi
+    along = (own % nz - gz % nz + nz) % nz
+    order = jnp.where(along == 0, 0, jnp.where(along <= nz // 2, 2 * along - 1, 2 * (nz - along)))
+    order = order * nx_hi + turn
+    order = n_gz - 1 - order if FAR else order
+    place = (order * CAPACITY + rank) * TILE + row_iota[0:1] % TILE
+
+    slot_iota = lax.broadcasted_iota(jnp.int32, (part_rows, rows), 0)
+    pl.semaphore_wait(barrier, n_gz + groups - 2)
 
     def permute(index):
-        first = pl.multiple_of(index * LANES, LANES)
+        first = pl.multiple_of(index * part_rows, LANES)
         chosen = jnp.where(slot_iota == place - first, 1.0, 0.0).astype(BF16)
         moved = lax.dot_general(chosen, x_buf[...], NT, preferred_element_type=F32)
-        send1[pl.ds(first, LANES)] = moved.astype(BF16)
-
-    loop(0, n_gz * slot_rows // LANES, permute)
-
-    pl.semaphore_wait(barrier, n_gz + groups - 2)
-    loop(1, n_gz, lambda k: copy1(k).start())
-    recv1[0:slot_rows] = send1[pl.ds(pl.multiple_of(gz * slot_rows, TILE), slot_rows)]
+        send1[pl.ds(first, part_rows)] = moved.astype(BF16)
+        loop(
+            jnp.maximum(index * part_slots, FIRST), jnp.minimum((index + 1) * part_slots, LAST),
+            lambda k: copy1(k).start(),
+        )
+
+    loop(0, parts, permute)
+    own_slot = OWN * slot_rows
+    recv1[own_slot : own_slot + slot_rows] = send1[own_slot : own_slot + slot_rows]
 
     acc[...] = jnp.zeros_like(acc)
-    y_iota = lax.broadcasted_iota(jnp.int32, (half + TILE, step), 0).astype(F32)
+    y_iota = (lax.broadcasted_iota(jnp.int32, (half + TILE, step), 0) - half // 2).astype(BF16)
     z_iota = lax.broadcasted_iota(jnp.int32, (TILE, step), 0)
     rim_x = z_iota // 2
-    rim_z = (z_iota % 2 + TILE).astype(F32)
-    z_iota = z_iota.astype(F32)
+    rim_z = (z_iota % 2 + TILE).astype(BF16)
+    z_iota = z_iota.astype(BF16)
 
     def spread_part(part, index):
-        e, first = index // (part_rows // step), index % (part_rows // step)
-        got = recv2[part, e, :, pl.ds(pl.multiple_of(first * step, step), step)].astype(F32)
-        plane = got[12:13]
-        y = got[13:14] + (half - 1.0)
+        got = recv2[part, :, pl.ds(pl.multiple_of(index * step, step), step)]
+        zero = jnp.zeros((), BF16)
+        y = got[13:14].astype(F32) + (half - 1.0)
         y = jnp.where(y < 0.0, y + ny, y)
         upper = y >= half
-        y = jnp.where(upper, y - half, y)
+        y = jnp.where(upper, y - half, y) - half // 2
+        ys = [(y + b).astype(BF16) for b in range(3)]
+        in_high = jnp.where(upper, 1.0, 0.0).astype(BF16)
+        got = got.astype(BF16)
+        z0 = got[12:13]
+        z1, z2 = z0 + 1, z0 + 2
         along_y = jnp.where(
-            y_iota == y, got[9:10],
-            jnp.where(y_iota == y + 1.0, got[10:11], jnp.where(y_iota == y + 2.0, got[11:12], 0.0)),
+            y_iota == ys[0], got[9:10],
+            jnp.where(y_iota == ys[1], got[10:11], jnp.where(y_iota == ys[2], got[11:12], zero)),
         ).astype(BF16)
         along_z = jnp.where(
-            z_iota == plane, got[6:7],
-            jnp.where(
-                z_iota == plane + 1.0, got[7:8], jnp.where(z_iota == plane + 2.0, got[8:9], 0.0)
-            ),
-        )
-        rim = jnp.where(
-            rim_z == plane + 1.0, got[7:8], jnp.where(rim_z == plane + 2.0, got[8:9], 0.0)
-        )
-        pieces = [along_z * got[s : s + 1] for s in range(2 * columns)]
+            z_iota == z0, got[6:7],
+            jnp.where(z_iota == z1, got[7:8], jnp.where(z_iota == z2, got[8:9], zero)),
+        )
+        rim = jnp.where(rim_z == z1, got[7:8], jnp.where(rim_z == z2, got[8:9], zero))
+        values = []
         for c in range(2):
-            value = jnp.zeros((TILE, step), F32)
+            value = jnp.zeros((TILE, step), BF16)
             for x in range(columns):
                 value = jnp.where(rim_x == x, got[2 * x + c : 2 * x + c + 1], value)
-            pieces.append(rim * value)
-        pieces = [jnp.where(upper, 0.0, piece) for piece in pieces] + [
-            jnp.where(upper, piece, 0.0) for piece in pieces
-        ]
+            values.append(value)
+        pieces = []
+        for mask in (1 - in_high, in_high):
+            z_part, rim_part = along_z * mask, rim * mask
+            pieces += [z_part * got[s : s + 1] for s in range(2 * columns)]
+            pieces += [rim_part * value for value in values]
         along_zx = jnp.concatenate([piece.astype(BF16) for piece in pieces], axis=0)
         acc[...] += lax.dot_general(along_y, along_zx, NT, preferred_element_type=F32)
 
     def take_part(part):
         def arrived(k):
             copy1(k).wait_recv()
-        loop(jnp.maximum(part * part_slots, 1), (part + 1) * part_slots, arrived)
+        loop(
+            jnp.maximum(part * part_slots, FIRST), jnp.minimum((part + 1) * part_slots, LAST), arrived
+        )
         first = pl.multiple_of(part * part_rows, TILE)
         turned = lax.dot_general(
-            pick_ref[...], recv1[pl.ds(first, part_rows)], NT, preferred_element_type=F32
+            small[0 : groups * TILE], recv1[pl.ds(first, part_rows)], NT, preferred_element_type=F32
         )
         send2[part] = turned.astype(BF16)
         loop(1, groups, lambda e: copy2(part, e).start())
-        recv2[part, 0] = send2[part, pl.ds(pl.multiple_of(my_group * TILE, TILE), TILE)]
+        recv2[part, :, 0:part_rows] = send2[part, pl.ds(pl.multiple_of(my_group * TILE, TILE), TILE)]
 
     def grid_part(part):
         loop(1, groups, lambda e: copy2(part, e).wait_recv())
@@ -232,11 +272,12 @@
         take_part(part)
         grid_part(part - 1)
 
+    fetches[5].wait()
     take_part(0)
     loop(1, parts, pipeline)
     grid_part(parts - 1)
 
-    table_copy.wait()
+    fetches[6].wait()
     lane = lax.broadcasted_iota(jnp.int32, (ny, LANES), 1)
     low, high = acc[:half, :LANES], acc[:half, LANES:]
     low_rim, high_rim = acc[half:, :LANES], acc[half:, LANES:]
@@ -255,13 +296,14 @@
     turned = turned + jnp.dot(table[1], both_high, preferred_element_type=F32)
     send3[...] = turned.astype(BF16)
 
-    loop(1, n_gz, lambda k: copy3(k).start())
+    mine3 = gz % nz * nx_hi + gz // nz
+    others(0, n_gz, mine3, lambda index: copy3(index).start())
     here = pl.ds(pl.multiple_of(gz * TILE, TILE), TILE)
     recv3[here] = send3[here]
-    loop(1, n_gz, lambda k: copy3(k).wait_recv())
+    others(0, n_gz, gz, lambda peer: arrival3(peer).wait_recv())
 
     got = recv3[...]
-    past = jnp.dot(got, rim_ref[...], preferred_element_type=F32)
+    past = jnp.dot(got, small[groups * TILE :], preferred_element_type=F32)
     planes = got.astype(F32) + jnp.concatenate([past[-TILE:], past[:-TILE]], axis=0)
     per = LANES // TILE
     spot = lax.broadcasted_iota(jnp.int32, (TILE, LANES), 1) // TILE
@@ -287,9 +329,9 @@
         out_ref[0, x] = real[:, :ny] - imag[:, ny:]
         out_ref[1, x] = real[:, ny:] + imag[:, :ny]
 
-    loop(1, n_gz, lambda k: copy1(k).wait_send())
+    loop(FIRST, LAST, lambda k: copy1(k).wait_send())
     loop(0, parts, lambda part: loop(1, groups, lambda e: copy2(part, e).wait_send()))
-    loop(1, n_gz, lambda k: copy3(k).wait_send())
+    others(0, n_gz, mine3, lambda index: copy3(index).wait_send())
 
 
 def local(sizes, pixels, taps, plane_offset, grid_row, slab_of_block):
@@ -302,14 +344,20 @@
     return pl.pallas_call(
         functools.partial(kernel, sizes),
         out_shape=jax.ShapeDtypeStruct((2, columns, ny // n_gz, ny), F32),
-        in_specs=[vmem] * 7 + [pl.BlockSpec(memory_space=pl.ANY)],
+        in_specs=[pl.BlockSpec(memory_space=pl.ANY)] * 7,
         out_specs=vmem,
         scratch_shapes=[
+            pltpu.VMEM((2, width, rows), BF16),
+            pltpu.VMEM((taps.shape[0], rows), BF16),
+            pltpu.VMEM((rows,), jnp.int32),
+            pltpu.VMEM((rows,), jnp.int32),
+            pltpu.VMEM((1, rows // TILE), jnp.int32),
+            pltpu.VMEM((groups * TILE + LANES, LANES), BF16),
             pltpu.VMEM((LANES, rows), BF16),
             pltpu.VMEM((slots, LANES), BF16),
             pltpu.VMEM((slots, LANES), BF16),
             pltpu.VMEM((parts, groups * TILE, slots // parts), BF16),
-            pltpu.VMEM((parts, groups, TILE, slots // parts), BF16),
+            pltpu.VMEM((parts, TILE, groups * slots // parts), BF16),
             pltpu.VMEM((ny // 2 + TILE, 2 * LANES), F32),
             pltpu.VMEM((2, ny, 2 * ny), BF16),
             pltpu.VMEM((ny, LANES), BF16),
@@ -320,19 +368,19 @@
             pltpu.SemaphoreType.DMA((parts, groups)),
             pltpu.SemaphoreType.DMA((n_gz,)),
             pltpu.SemaphoreType.DMA((n_gz,)),
-            pltpu.SemaphoreType.DMA,
+            pltpu.SemaphoreType.DMA((7,)),
         ],
         compiler_params=pltpu.CompilerParams(
-            collective_id=0, has_side_effects=True, vmem_limit_bytes=48 * 1024 * 1024
+            collective_id=0, has_side_effects=True, vmem_limit_bytes=64 * 1024 * 1024
         ),
     )(
-        pixels, taps, plane_offset.reshape(1, rows), grid_row.reshape(1, rows), slab_of_block,
-        jnp.asarray(pick_table(width, groups)), jnp.asarray(rim_table(columns)),
+        pixels, taps, plane_offset, grid_row, slab_of_block.reshape(1, rows // TILE),
+        jnp.asarray(np.concatenate([pick_table(width, groups), rim_table(columns)])),
         jnp.asarray(transform_table(ny)),
     )
 
 
-def solution(mesh, width=48, ny=512, parts=4, step=384):
+def solution(mesh, width=48, ny=512, parts=4, step=3072):
     sizes = (mesh.shape["img"], mesh.shape["gz"], mesh.shape["gy"], width, ny, parts, step)
     return jax.shard_map(
         functools.partial(local, sizes),

time: 79.1 us -> 66.6 us (0.84)
  Pallas kernels: 71.1 us -> 64.9 us
  local copies, waits for them, and re-layouts: 7.63 us -> 1.62 us
    pallas_call x1, Pallas kernels: 71.1 us -> 64.9 us  [local(): pl.pallas_call(functools.partial(kernel, sizes), out_shape=jax.ShapeDtype...]
    unnamed x12 -> x1, local copies, waits for them, and re-layouts: 6.25 us -> 1.62 us
    reshape x2 -> x0, local copies, waits for them, and re-layouts: 1.38 us -> none  [the longest x1 0.69 us: local(): plane_offset.reshape(1, rows)]
where the time goes in v1:
time: 66.6 us; the launch traced here: 66.5 us
  Pallas kernels  64.9 us (97%)
  local copies, waits for them, and re-layouts  1.62 us (2%)
    pallas_call x1, Pallas kernels, local(): pl.pallas_call(functools.partial(kernel, sizes), out_shape=jax.ShapeDtype...  64.9 us
    unnamed x1, local copies, waits for them, and re-layouts  1.62 us

profile of v1, /device:TPU:1, one launch (start us, length us, event | category | flops | bytes accessed | tf_op | source)
XLA Modules:
  0.0 66.5 jit_solution(2041782278950392721)
XLA Ops:
  0.0 64.9 %shard_map.73 = f32[2,3,16,512]{3,2,1,0:T(8,128)} custom-call(bf16[2,48,768]{2,1,0:T(8,128)(2,1)} %pix_hbm.1, bf16[9,768]{1,0:T(8,128)(2,1)} %taps_hbm.1, s32[768]{0:T(1024)} %plane_hbm.1, s32[768]{0:T(1024)} %row_hbm.1, s32[1,48]{1,0:T(1,128)} %bitcast.1, bf16[384,128]{1,0:T(8,128)(2,1)} %constant.4.clone.small_hbm, ...), custom_call_target="tpu_custom_call" | custom-call | tf_op jit(solution)/shard_map/pallas_call | solution.py:344
  64.9 1.6 %copy.9 = f32[2,3,16,512]{3,2,1,0:T(8,128)} copy(f32[2,3,16,512]{3,2,1,0:T(8,128)} %shard_map.73) | data formatting | bytes 393216

commit v2 on v1

--- a/solution.py
+++ b/solution.py
@@ -65,32 +65,42 @@
     part_slots = n_gz // parts
     part_rows = part_slots * slot_rows
     half = ny // 2
-    FAR, FIRST, LAST, OWN = True, 0, n_gz - 1, n_gz - 1
+    reach = nz // 2
+    sends = n_gz // 2
+    own_send = sends - nx_hi
 
     img, gz, gy = lax.axis_index("img"), lax.axis_index("gz"), lax.axis_index("gy")
     my_group = img * n_gy + gy
 
+    my_x, my_z = lax.div(gz, nz), lax.rem(gz, nz)
+    my_y, my_side = lax.div(img, 2), lax.rem(img, 2)
+
     def slab_peer(k):
-        k = n_gz - 1 - k if FAR else k
-        turn, m = k % nx_hi, k // nx_hi
-        along = ((m + 1) // 2) * (2 * (m % 2) - 1)
-        z = (gz % nz + along + nz) % nz
-        x = (gz // nz + turn) % nx_hi
-        return x * nz + z
+        turn, m = k % sends % nx_hi, k % sends // nx_hi
+        x = lax.rem(my_x + turn, nx_hi)
+        along = (reach - m) // 2 * (2 * (m % 2) - 1) + nz
+        z = my_z + along + (x * reach if m == 0 else 0)
+        return x * nz + lax.rem(z, nz)
+
+    def any_peer(k):
+        turn, m = k % nx_hi, nz - 1 - k // nx_hi
+        along = (m + 1) // 2 * (2 * (m % 2) - 1) + nz
+        return lax.rem(my_x + turn, nx_hi) * nz + lax.rem(my_z + along, nz)
+
+    any_own = n_gz - nx_hi
+    any_others = [k for k in range(n_gz) if k != any_own]
 
     def group_peer(e):
-        core, rest = e % n_gy, e // n_gy
-        side, along = rest % 2, rest // 2
-        y = (img // 2 + along) % (n_img // 2)
-        x = (img % 2 + side) % 2
-        return y * 2 + x, (gy + core) % n_gy
+        core, side, along = e % n_gy, e // n_gy % 2, e // n_gy // 2
+        y = lax.rem(my_y + along, n_img // 2)
+        return y * 2 + lax.rem(my_side + side, 2), lax.rem(gy + core, n_gy)
 
     def copy1(k):
         peer = slab_peer(k)
         return pltpu.make_async_remote_copy(
             src_ref=send1.at[pl.ds(pl.multiple_of(k * slot_rows, TILE), slot_rows)],
             dst_ref=recv1.at[pl.ds(pl.multiple_of(k * slot_rows, TILE), slot_rows)],
-            send_sem=s1_sem.at[k], recv_sem=r1_sem.at[k],
+            send_sem=s1_sem.at[0], recv_sem=r1_sem.at[k // part_slots],
             device_id=(img, peer, gy), device_id_type=MESH,
         )
 
@@ -100,24 +110,18 @@
         return pltpu.make_async_remote_copy(
             src_ref=send2.at[part, pl.ds(pl.multiple_of(peer * TILE, TILE), TILE)],
             dst_ref=recv2.at[part, :, pl.ds(pl.multiple_of(e * part_rows, LANES), part_rows)],
-            send_sem=s2_sem.at[part, e], recv_sem=r2_sem.at[part, e],
+            send_sem=s2_sem.at[0], recv_sem=r2_sem.at[part],
             device_id=(to_img, gz, to_gy), device_id_type=MESH,
         )
 
-    def copy3(index):
-        peer = index % nx_hi * nz + index // nx_hi
+    def copy3(slab, k):
+        peer = any_peer(k)
         return pltpu.make_async_remote_copy(
-            src_ref=send3.at[pl.ds(pl.multiple_of(peer * TILE, TILE), TILE)],
-            dst_ref=recv3.at[pl.ds(pl.multiple_of(gz * TILE, TILE), TILE)],
-            send_sem=s3_sem.at[peer], recv_sem=r3_sem.at[gz],
+            src_ref=send3.at[slab, pl.ds(pl.multiple_of(peer * TILE, TILE), TILE)],
+            dst_ref=recv3.at[slab, pl.ds(pl.multiple_of(gz * TILE, TILE), TILE)],
+            send_sem=s3_sem.at[0], recv_sem=r3_sem.at[slab],
             device_id=(img, peer, gy), device_id_type=MESH,
         )
-
-    def loop(first, last, do):
-        def body(index, carry):
-            do(index)
-            return carry
-        lax.fori_loop(first, last, body, 0)
 
     pairs = [
         (slab_hbm, slab_ref), (taps_hbm, taps_ref), (plane_hbm, plane_ref), (row_hbm, row_ref),
@@ -127,32 +131,33 @@
     for fetch in fetches:
         fetch.start()
 
-    def arrival3(peer):
-        here = recv3.at[pl.ds(pl.multiple_of(peer * TILE, TILE), TILE)]
-        return pltpu.make_async_remote_copy(
-            src_ref=here, dst_ref=here, send_sem=s3_sem.at[0], recv_sem=r3_sem.at[peer],
-            device_id=(img, peer, gy), device_id_type=MESH,
-        )
-
-    def others(first, last, mine, do):
-        def step_of(index):
-            @pl.when(index != mine)
-            def _():
-                do(index)
-        loop(first, last, step_of)
+    def landed(view, sem):
+        pltpu.make_async_remote_copy(
+            src_ref=view, dst_ref=view, send_sem=s1_sem.at[0], recv_sem=sem,
+            device_id=(img, any_peer(0), gy), device_id_type=MESH,
+        ).wait_recv()
+
+    def left(view, sem):
+        pltpu.make_async_remote_copy(
+            src_ref=view, dst_ref=view, send_sem=sem, recv_sem=r1_sem.at[0],
+            device_id=(img, any_peer(0), gy), device_id_type=MESH,
+        ).wait_send()
+
+    def loop(first, last, do):
+        def body(index, carry):
+            do(index)
+            return carry
+        lax.fori_loop(first, last, body, 0)
 
     barrier = pltpu.get_barrier_semaphore()
 
-    def greet_slab(k):
-        pl.semaphore_signal(barrier, inc=1, device_id=(img, slab_peer(k), gy), device_id_type=MESH)
-
-    def greet_group(e):
+    for k in any_others:
+        pl.semaphore_signal(
+            barrier, inc=1, device_id=(img, any_peer(k), gy), device_id_type=MESH
+        )
+    for e in range(1, groups):
         to_img, to_gy = group_peer(e)
         pl.semaphore_signal(barrier, inc=1, device_id=(to_img, gz, to_gy), device_id_type=MESH)
-
-    loop(FIRST, LAST, greet_slab)
-    loop(1, groups, greet_group)
-
 
     for fetch in fetches[:5]:
         fetch.wait()
@@ -184,29 +189,34 @@
     own = jnp.sum(jnp.where(block_iota == row_block, target, 0), axis=0, keepdims=True)
     earlier = jnp.where((target == own) & (block_iota < row_block), 1, 0)
     rank = jnp.sum(earlier, axis=0, keepdims=True)
-    turn = (own // nz - gz // nz + nx_hi) % nx_hi
-    along = (own % nz - gz % nz + nz) % nz
-    order = jnp.where(along == 0, 0, jnp.where(along <= nz // 2, 2 * along - 1, 2 * (nz - along)))
-    order = order * nx_hi + turn
-    order = n_gz - 1 - order if FAR else order
+    side = own // nz
+    turn = (side - gz // nz + nx_hi) % nx_hi
+    along = (own % nz - gz % nz + nz + reach // 2 - side + nz) % nz
+    far_owner = along // reach
+    along = along % reach - reach // 2 + side
+    order = jnp.where(along >= 0, jnp.maximum(reach - 1 - 2 * along, 0), reach + 2 * along)
+    order = far_owner * sends + order * nx_hi + turn
     place = (order * CAPACITY + rank) * TILE + row_iota[0:1] % TILE
 
     slot_iota = lax.broadcasted_iota(jnp.int32, (part_rows, rows), 0)
     pl.semaphore_wait(barrier, n_gz + groups - 2)
 
+    def part_sends(part):
+        every = range(part * part_slots, (part + 1) * part_slots)
+        return [k for k in every if k % sends != own_send]
+
     def permute(index):
-        first = pl.multiple_of(index * part_rows, LANES)
+        first = index * part_rows
         chosen = jnp.where(slot_iota == place - first, 1.0, 0.0).astype(BF16)
         moved = lax.dot_general(chosen, x_buf[...], NT, preferred_element_type=F32)
-        send1[pl.ds(first, part_rows)] = moved.astype(BF16)
-        loop(
-            jnp.maximum(index * part_slots, FIRST), jnp.minimum((index + 1) * part_slots, LAST),
-            lambda k: copy1(k).start(),
-        )
-
-    loop(0, parts, permute)
-    own_slot = OWN * slot_rows
-    recv1[own_slot : own_slot + slot_rows] = send1[own_slot : own_slot + slot_rows]
+        send1[first : first + part_rows] = moved.astype(BF16)
+        for k in part_sends(index):
+            copy1(k).start()
+
+    for part in range(parts):
+        permute(part)
+    for k in (own_send, own_send + sends):
+        recv1[k * slot_rows : (k + 1) * slot_rows] = send1[k * slot_rows : (k + 1) * slot_rows]
 
     acc[...] = jnp.zeros_like(acc)
     y_iota = (lax.broadcasted_iota(jnp.int32, (half + TILE, step), 0) - half // 2).astype(BF16)
@@ -248,63 +258,74 @@
             pieces += [z_part * got[s : s + 1] for s in range(2 * columns)]
             pieces += [rim_part * value for value in values]
         along_zx = jnp.concatenate([piece.astype(BF16) for piece in pieces], axis=0)
-        acc[...] += lax.dot_general(along_y, along_zx, NT, preferred_element_type=F32)
+        acc[part // (parts // 2)] += lax.dot_general(along_y, along_zx, NT, preferred_element_type=F32)
 
     def take_part(part):
-        def arrived(k):
-            copy1(k).wait_recv()
-        loop(
-            jnp.maximum(part * part_slots, FIRST), jnp.minimum((part + 1) * part_slots, LAST), arrived
-        )
-        first = pl.multiple_of(part * part_rows, TILE)
+        landed(recv1.at[pl.ds(0, len(part_sends(part)) * slot_rows)], r1_sem.at[part])
+        first = part * part_rows
         turned = lax.dot_general(
-            small[0 : groups * TILE], recv1[pl.ds(first, part_rows)], NT, preferred_element_type=F32
+            small[0 : groups * TILE], recv1[first : first + part_rows], NT, preferred_element_type=F32
         )
         send2[part] = turned.astype(BF16)
-        loop(1, groups, lambda e: copy2(part, e).start())
+        for e in range(1, groups):
+            copy2(part, e).start()
         recv2[part, :, 0:part_rows] = send2[part, pl.ds(pl.multiple_of(my_group * TILE, TILE), TILE)]
 
     def grid_part(part):
-        loop(1, groups, lambda e: copy2(part, e).wait_recv())
+        landed(recv2.at[part, :, pl.ds(0, (groups - 1) * part_rows)], r2_sem.at[part])
         loop(0, groups * part_rows // step, functools.partial(spread_part, part))
 
-    def pipeline(part):
+    lane = lax.broadcasted_iota(jnp.int32, (ny, LANES), 1)
+    here = pl.ds(pl.multiple_of(gz * TILE, TILE), TILE)
+
+    def turn_y(slab):
+        low, high = acc[slab, :half, :LANES], acc[slab, :half, LANES:]
+        low_rim, high_rim = acc[slab, half:, :LANES], acc[slab, half:, LANES:]
+        grid = jnp.concatenate(
+            [low[:TILE] + high_rim, low[TILE:], high[:TILE] + low_rim, high[TILE:]], axis=0
+        )
+        other = jnp.where(
+            (lane // TILE) % 2 == 0, -pltpu.roll(grid, LANES - TILE, 1), pltpu.roll(grid, TILE, 1)
+        )
+        both = jnp.concatenate([grid, other], axis=0)
+        both_high = both.astype(BF16)
+        both_low = (both - both_high.astype(F32)).astype(BF16)
+        both_bits = jnp.concatenate([both_high, both_low], axis=1)
+        wide = jnp.dot(table[0], both_bits, preferred_element_type=F32)
+        turned = wide[:, :LANES] + wide[:, LANES:]
+        turned = turned + jnp.dot(table[1], both_high, preferred_element_type=F32)
+        send3[slab] = turned.astype(BF16)
+        for k in any_others:
+            copy3(slab, k).start()
+        recv3[slab, here] = send3[slab, here]
+
+    fetches[5].wait()
+    fetches[6].wait()
+    per_slab = parts // 2
+    for part in range(parts):
         take_part(part)
-        grid_part(part - 1)
-
-    fetches[5].wait()
-    take_part(0)
-    loop(1, parts, pipeline)
-    grid_part(parts - 1)
-
-    fetches[6].wait()
-    lane = lax.broadcasted_iota(jnp.int32, (ny, LANES), 1)
-    low, high = acc[:half, :LANES], acc[:half, LANES:]
-    low_rim, high_rim = acc[half:, :LANES], acc[half:, LANES:]
-    grid = jnp.concatenate(
-        [low[:TILE] + high_rim, low[TILE:], high[:TILE] + low_rim, high[TILE:]], axis=0
-    )
-    other = jnp.where(
-        (lane // TILE) % 2 == 0, -pltpu.roll(grid, LANES - TILE, 1), pltpu.roll(grid, TILE, 1)
-    )
-    both = jnp.concatenate([grid, other], axis=0)
-    both_high = both.astype(BF16)
-    both_low = (both - both_high.astype(F32)).astype(BF16)
-    both_bits = jnp.concatenate([both_high, both_low], axis=1)
-    wide = jnp.dot(table[0], both_bits, preferred_element_type=F32)
-    turned = wide[:, :LANES] + wide[:, LANES:]
-    turned = turned + jnp.dot(table[1], both_high, preferred_element_type=F32)
-    send3[...] = turned.astype(BF16)
-
-    mine3 = gz % nz * nx_hi + gz // nz
-    others(0, n_gz, mine3, lambda index: copy3(index).start())
-    here = pl.ds(pl.multiple_of(gz * TILE, TILE), TILE)
-    recv3[here] = send3[here]
-    others(0, n_gz, gz, lambda peer: arrival3(peer).wait_recv())
-
-    got = recv3[...]
-    past = jnp.dot(got, small[groups * TILE :], preferred_element_type=F32)
-    planes = got.astype(F32) + jnp.concatenate([past[-TILE:], past[:-TILE]], axis=0)
+
+    def slab_step(slab):
+        grid_part(slab * per_slab)
+
+        loop(slab * per_slab + 1, (slab + 1) * per_slab, grid_part)
+        turn_y(slab)
+
+    loop(0, 2, slab_step)
+    left(send1.at[pl.ds(0, (n_gz - 2) * slot_rows)], s1_sem.at[0])
+    left(recv2.at[:, :, pl.ds(0, (groups - 1) * part_rows)], s2_sem.at[0])
+    for slab in range(2):
+        landed(recv3.at[slab, pl.ds(0, (n_gz - 1) * TILE)], r3_sem.at[slab])
+    left(recv3.at[:, pl.ds(0, (n_gz - 1) * TILE)], s3_sem.at[0])
+
+    got = recv3[0]
+    span = reach * TILE
+    swapped = [recv3[1, (2 * x + 1 - i) * span : (2 * x + 2 - i) * span] for x in range(nx_hi) for i in range(2)]
+    swapped = jnp.concatenate(swapped, axis=0)
+    place_rim = small[groups * TILE :]
+    past = jnp.dot(got, place_rim, preferred_element_type=F32)
+    past = past + jnp.dot(swapped, place_rim, preferred_element_type=F32)
+    planes = got.astype(F32) + swapped.astype(F32) + jnp.concatenate([past[-TILE:], past[:-TILE]], axis=0)
     per = LANES // TILE
     spot = lax.broadcasted_iota(jnp.int32, (TILE, LANES), 1) // TILE
     ordered = []
@@ -318,20 +339,21 @@
                 turn = (j - s) * TILE % LANES
                 tile = pltpu.roll(tile, turn, 1) if turn else tile
                 value = jnp.where(spot == j, tile, value)
-            across.append(value.astype(BF16))
+            across.append(value)
         ordered.append(jnp.concatenate(across, axis=1))
     ordered = jnp.concatenate(ordered, axis=0)
-    volume = jnp.dot(ordered, table[0], preferred_element_type=F32)
-    volume = volume + jnp.dot(ordered, table[1], preferred_element_type=F32)
+    ordered_high = ordered.astype(BF16)
+    ordered_low = (ordered - ordered_high.astype(F32)).astype(BF16)
+    ordered_bits = jnp.concatenate([ordered_high, ordered_low], axis=0)
+    lines = ordered.shape[0]
+    wide = jnp.dot(ordered_bits, table[0], preferred_element_type=F32)
+    volume = wide[:lines] + wide[lines:]
+    volume = volume + jnp.dot(ordered_high, table[1], preferred_element_type=F32)
     for x in range(columns):
         real = volume[2 * x * TILE : (2 * x + 1) * TILE]
         imag = volume[(2 * x + 1) * TILE : (2 * x + 2) * TILE]
         out_ref[0, x] = real[:, :ny] - imag[:, ny:]
         out_ref[1, x] = real[:, ny:] + imag[:, :ny]
-
-    loop(FIRST, LAST, lambda k: copy1(k).wait_send())
-    loop(0, parts, lambda part: loop(1, groups, lambda e: copy2(part, e).wait_send()))
-    others(0, n_gz, mine3, lambda index: copy3(index).wait_send())
 
 
 def local(sizes, pixels, taps, plane_offset, grid_row, slab_of_block):
@@ -358,16 +380,16 @@
             pltpu.VMEM((slots, LANES), BF16),
             pltpu.VMEM((parts, groups * TILE, slots // parts), BF16),
             pltpu.VMEM((parts, TILE, groups * slots // parts), BF16),
-            pltpu.VMEM((ny // 2 + TILE, 2 * LANES), F32),
+            pltpu.VMEM((2, ny // 2 + TILE, 2 * LANES), F32),
             pltpu.VMEM((2, ny, 2 * ny), BF16),
-            pltpu.VMEM((ny, LANES), BF16),
-            pltpu.VMEM((ny, LANES), BF16),
-            pltpu.SemaphoreType.DMA((n_gz,)),
-            pltpu.SemaphoreType.DMA((n_gz,)),
-            pltpu.SemaphoreType.DMA((parts, groups)),
-            pltpu.SemaphoreType.DMA((parts, groups)),
-            pltpu.SemaphoreType.DMA((n_gz,)),
-            pltpu.SemaphoreType.DMA((n_gz,)),
+            pltpu.VMEM((2, ny, LANES), BF16),
+            pltpu.VMEM((2, ny, LANES), BF16),
+            pltpu.SemaphoreType.DMA((1,)),
+            pltpu.SemaphoreType.DMA((parts,)),
+            pltpu.SemaphoreType.DMA((1,)),
+            pltpu.SemaphoreType.DMA((parts,)),
+            pltpu.SemaphoreType.DMA((1,)),
+            pltpu.SemaphoreType.DMA((2,)),
             pltpu.SemaphoreType.DMA((7,)),
         ],
         compiler_params=pltpu.CompilerParams(

time: 66.6 us -> 55.9 us (0.84)
  Pallas kernels: 64.9 us -> 54.1 us
    pallas_call x1, Pallas kernels: 64.9 us -> 54.1 us  [local(): pl.pallas_call(functools.partial(kernel, sizes), out_shape=jax.ShapeDtype...]
where the time goes in v2:
time: 55.9 us; the launch traced here: 55.7 us
  Pallas kernels  54.1 us (97%)
  local copies, waits for them, and re-layouts  1.62 us (3%)
    pallas_call x1, Pallas kernels, local(): pl.pallas_call(functools.partial(kernel, sizes), out_shape=jax.ShapeDtype...  54.1 us
    unnamed x1, local copies, waits for them, and re-layouts  1.62 us

profile of v2, /device:TPU:1, one launch (start us, length us, event | category | flops | bytes accessed | tf_op | source)
XLA Modules:
  0.0 55.7 jit_solution(13487932177188393624)
XLA Ops:
  0.0 54.1 %shard_map.73 = f32[2,3,16,512]{3,2,1,0:T(8,128)} custom-call(bf16[2,48,768]{2,1,0:T(8,128)(2,1)} %pix_hbm.1, bf16[9,768]{1,0:T(8,128)(2,1)} %taps_hbm.1, s32[768]{0:T(1024)} %plane_hbm.1, s32[768]{0:T(1024)} %row_hbm.1, s32[1,48]{1,0:T(1,128)} %bitcast.1, bf16[384,128]{1,0:T(8,128)(2,1)} %constant.4.clone.small_hbm, ...), custom_call_target="tpu_custom_call" | custom-call | tf_op jit(solution)/shard_map/pallas_call | solution.py:366
  54.1 1.6 %copy.9 = f32[2,3,16,512]{3,2,1,0:T(8,128)} copy(f32[2,3,16,512]{3,2,1,0:T(8,128)} %shard_map.73) | data formatting | bytes 393216

commit v3 on v2

--- a/solution.py
+++ b/solution.py
@@ -114,8 +114,7 @@
             device_id=(to_img, gz, to_gy), device_id_type=MESH,
         )
 
-    def copy3(slab, k):
-        peer = any_peer(k)
+    def copy3(slab, peer):
         return pltpu.make_async_remote_copy(
             src_ref=send3.at[slab, pl.ds(pl.multiple_of(peer * TILE, TILE), TILE)],
             dst_ref=recv3.at[slab, pl.ds(pl.multiple_of(gz * TILE, TILE), TILE)],
@@ -151,7 +150,8 @@
 
     barrier = pltpu.get_barrier_semaphore()
 
-    for k in any_others:
+    near = [k for k in any_others if nz - 1 - k // nx_hi <= reach]
+    for k in near:
         pl.semaphore_signal(
             barrier, inc=1, device_id=(img, any_peer(k), gy), device_id_type=MESH
         )
@@ -199,7 +199,7 @@
     place = (order * CAPACITY + rank) * TILE + row_iota[0:1] % TILE
 
     slot_iota = lax.broadcasted_iota(jnp.int32, (part_rows, rows), 0)
-    pl.semaphore_wait(barrier, n_gz + groups - 2)
+    pl.semaphore_wait(barrier, len(near) + groups - 1)
 
     def part_sends(part):
         every = range(part * part_slots, (part + 1) * part_slots)
@@ -295,8 +295,13 @@
         turned = wide[:, :LANES] + wide[:, LANES:]
         turned = turned + jnp.dot(table[1], both_high, preferred_element_type=F32)
         send3[slab] = turned.astype(BF16)
-        for k in any_others:
-            copy3(slab, k).start()
+        for z in range(nz):
+            for x in range(nx_hi):
+                peer = x * nz + z
+
+                @pl.when(gz != peer)
+                def _():
+                    copy3(slab, peer).start()
         recv3[slab, here] = send3[slab, here]
 
     fetches[5].wait()

time: 55.9 us -> 52.9 us (0.946)
  the two profiles are of different devices: /device:TPU:1 before, /device:TPU:32 now
where the time goes in v3:
time: 52.9 us; the launch traced here: 52.7 us
  Pallas kernels  51.1 us (97%)
  local copies, waits for them, and re-layouts  1.62 us (3%)
    pallas_call x1, Pallas kernels, local(): pl.pallas_call(functools.partial(kernel, sizes), out_shape=jax.ShapeDtype...  51.1 us
    unnamed x1, local copies, waits for them, and re-layouts  1.62 us

profile of v3, /device:TPU:32, one launch (start us, length us, event | category | flops | bytes accessed | tf_op | source)
XLA Modules:
  0.0 52.7 jit_solution(12488544138419573430)
XLA Ops:
  0.0 51.1 %shard_map.73 = f32[2,3,16,512]{3,2,1,0:T(8,128)} custom-call(bf16[2,48,768]{2,1,0:T(8,128)(2,1)} %pix_hbm.1, bf16[9,768]{1,0:T(8,128)(2,1)} %taps_hbm.1, s32[768]{0:T(1024)} %plane_hbm.1, s32[768]{0:T(1024)} %row_hbm.1, s32[1,48]{1,0:T(1,128)} %bitcast.1, bf16[384,128]{1,0:T(8,128)(2,1)} %constant.4.clone.small_hbm, ...), custom_call_target="tpu_custom_call" | custom-call | tf_op jit(solution)/shard_map/pallas_call | solution.py:371
  51.1 1.6 %copy.9 = f32[2,3,16,512]{3,2,1,0:T(8,128)} copy(f32[2,3,16,512]{3,2,1,0:T(8,128)} %shard_map.73) | data formatting | bytes 393216

commit v4 on v3

--- a/solution.py
+++ b/solution.py
@@ -199,7 +199,6 @@
     place = (order * CAPACITY + rank) * TILE + row_iota[0:1] % TILE
 
     slot_iota = lax.broadcasted_iota(jnp.int32, (part_rows, rows), 0)
-    pl.semaphore_wait(barrier, len(near) + groups - 1)
 
     def part_sends(part):
         every = range(part * part_slots, (part + 1) * part_slots)
@@ -210,6 +209,8 @@
         chosen = jnp.where(slot_iota == place - first, 1.0, 0.0).astype(BF16)
         moved = lax.dot_general(chosen, x_buf[...], NT, preferred_element_type=F32)
         send1[first : first + part_rows] = moved.astype(BF16)
+        if index == 0:
+            pl.semaphore_wait(barrier, len(near) + groups - 1)
         for k in part_sends(index):
             copy1(k).start()
 
@@ -267,7 +268,7 @@
             small[0 : groups * TILE], recv1[first : first + part_rows], NT, preferred_element_type=F32
         )
         send2[part] = turned.astype(BF16)
-        for e in range(1, groups):
+        for e in reversed(range(1, groups)):
             copy2(part, e).start()
         recv2[part, :, 0:part_rows] = send2[part, pl.ds(pl.multiple_of(my_group * TILE, TILE), TILE)]
 
@@ -295,13 +296,21 @@
         turned = wide[:, :LANES] + wide[:, LANES:]
         turned = turned + jnp.dot(table[1], both_high, preferred_element_type=F32)
         send3[slab] = turned.astype(BF16)
-        for z in range(nz):
-            for x in range(nx_hi):
-                peer = x * nz + z
-
-                @pl.when(gz != peer)
-                def _():
-                    copy3(slab, peer).start()
+        @pl.when(slab == 0)
+        def _():
+            for k in any_others:
+                copy3(0, any_peer(k)).start()
+
+        @pl.when(slab == 1)
+        def _():
+            for z in range(nz):
+                for x in range(nx_hi):
+                    peer = x * nz + z
+
+                    @pl.when(gz != peer)
+                    def _():
+                        copy3(1, peer).start()
+
         recv3[slab, here] = send3[slab, here]
 
     fetches[5].wait()
@@ -319,16 +328,15 @@
     loop(0, 2, slab_step)
     left(send1.at[pl.ds(0, (n_gz - 2) * slot_rows)], s1_sem.at[0])
     left(recv2.at[:, :, pl.ds(0, (groups - 1) * part_rows)], s2_sem.at[0])
-    for slab in range(2):
-        landed(recv3.at[slab, pl.ds(0, (n_gz - 1) * TILE)], r3_sem.at[slab])
-    left(recv3.at[:, pl.ds(0, (n_gz - 1) * TILE)], s3_sem.at[0])
-
+
+    landed(recv3.at[0, pl.ds(0, (n_gz - 1) * TILE)], r3_sem.at[0])
     got = recv3[0]
+    place_rim = small[groups * TILE :]
+    past = jnp.dot(got, place_rim, preferred_element_type=F32)
+    landed(recv3.at[1, pl.ds(0, (n_gz - 1) * TILE)], r3_sem.at[1])
     span = reach * TILE
     swapped = [recv3[1, (2 * x + 1 - i) * span : (2 * x + 2 - i) * span] for x in range(nx_hi) for i in range(2)]
     swapped = jnp.concatenate(swapped, axis=0)
-    place_rim = small[groups * TILE :]
-    past = jnp.dot(got, place_rim, preferred_element_type=F32)
     past = past + jnp.dot(swapped, place_rim, preferred_element_type=F32)
     planes = got.astype(F32) + swapped.astype(F32) + jnp.concatenate([past[-TILE:], past[:-TILE]], axis=0)
     per = LANES // TILE
@@ -359,6 +367,7 @@
         imag = volume[(2 * x + 1) * TILE : (2 * x + 2) * TILE]
         out_ref[0, x] = real[:, :ny] - imag[:, ny:]
         out_ref[1, x] = real[:, ny:] + imag[:, :ny]
+    left(recv3.at[:, pl.ds(0, (n_gz - 1) * TILE)], s3_sem.at[0])
 
 
 def local(sizes, pixels, taps, plane_offset, grid_row, slab_of_block):

time: 52.9 us -> 51.8 us (0.979)
  the two profiles are of different devices: /device:TPU:32 before, /device:TPU:1 now
where the time goes in v4:
time: 51.8 us; the launch traced here: 50.9 us
  Pallas kernels  49.3 us (95%)
  local copies, waits for them, and re-layouts  1.62 us (3%)
    pallas_call x1, Pallas kernels, local(): pl.pallas_call(functools.partial(kernel, sizes), out_shape=jax.ShapeDtype...  49.3 us
    unnamed x1, local copies, waits for them, and re-layouts  1.62 us

profile of v4, /device:TPU:1, one launch (start us, length us, event | category | flops | bytes accessed | tf_op | source)
XLA Modules:
  0.0 50.9 jit_solution(9227005252889320712)
XLA Ops:
  0.0 49.3 %shard_map.73 = f32[2,3,16,512]{3,2,1,0:T(8,128)} custom-call(bf16[2,48,768]{2,1,0:T(8,128)(2,1)} %pix_hbm.1, bf16[9,768]{1,0:T(8,128)(2,1)} %taps_hbm.1, s32[768]{0:T(1024)} %plane_hbm.1, s32[768]{0:T(1024)} %row_hbm.1, s32[1,48]{1,0:T(1,128)} %bitcast.1, bf16[384,128]{1,0:T(8,128)(2,1)} %constant.4.clone.small_hbm, ...), custom_call_target="tpu_custom_call" | custom-call | tf_op jit(solution)/shard_map/pallas_call | solution.py:380
  49.3 1.6 %copy.9 = f32[2,3,16,512]{3,2,1,0:T(8,128)} copy(f32[2,3,16,512]{3,2,1,0:T(8,128)} %shard_map.73) | data formatting | bytes 393216
